TPU v7x, 32 devices: a whole 2x2x4 slice. The times are simulated.
32 devices in a mesh: site: 8 (over y, x, core), real: 4 (over z).
Axes of the slice: x: 2, y: 2, z: 4, core: 2. Of those that a mesh axis runs over, the one named last changes fastest.
Arguments:
- field: float32 [64, 16384], P('real', 'site'), may hold values from -6 to 6
- observed: float32 [20480], P('site'), may hold values from -6 to 6
- inv_cov: float32 [20480, 20480], P('site', 'real'), may hold values from -0.0012207031 to 0.0012207031
- site_xy: float32 [2, 16384], P(None, 'site'), may hold values from 0 to 200
- station_site: int32 [20480], P('site'), may hold values from 0 to 16383, as said below
- site_mean: float32 [16384], P('site'), may hold values from -3 to 0
- building_site: int32 [32768], P('site'), may hold values from 0 to 16383, as said below
- building_class: int32 [32768], P('site'), may hold values from 0 to 35
- building_tract: int32 [32768], P('site'), may hold values from 0 to 4095
- building_value: float32 [32768], P('site')
- median_ln: float32 [4, 36], replicated, may hold values from -2.3 to 0.4
- beta_ln: float32 [36], replicated, may hold values from 0.4 to 0.8
- loss_step: float32 [4, 36], replicated, may hold values from 0.02 to 0.3
Outputs:
- cond_field: float32 [64, 16384], P('real', 'site')
- tract_loss: float32 [64, 4096], P('real', 'site')
- total_loss: float32 [64], P('real')
Inputs may be any that keep to these rules, and one draw needn't show every extreme that they name: `station_site`: the stations of rows d * 2560 to (d + 1) * 2560 - 1 stand at sites d * 2048 to (d + 1) * 2048 - 1; several stations may share a site. `building_site`: the buildings of rows d * 4096 to (d + 1) * 4096 - 1 stand at sites d * 2048 to (d + 1) * 2048 - 1.
All inputs are finite; a program needn't handle non-finite values.
Results may differ from a plain program's by a relative error of at most 0.003.
Values may be sent and summed in bfloat16 or wider, within the bound.
A program may use at most 128 MiB of HBM per device.

v0:
```python
import math

import jax
import jax.numpy as jnp
from jax import lax
from jax.sharding import PartitionSpec as P

TRACT_DEV = 512


def normal_cdf(value):
    return 0.5 * (1.0 + lax.erf(value * 0.7071067811865476))


def shards(
    field,
    observed,
    inv_cov,
    site_xy,
    station_site,
    site_mean,
    building_site,
    building_class,
    building_tract,
    building_value,
    median_ln,
    beta_ln,
    loss_step,
):
    real_rows = field.shape[0]
    site_block = field.shape[1]
    site_count = lax.axis_size("site")
    first_site = lax.axis_index("site") * site_block
    station_local = station_site - first_site
    station_field = jnp.take(field, station_local, axis=1)
    innov = observed[None, :] - station_field
    partial_w = jnp.dot(
        lax.all_gather(innov, "real", axis=0, tiled=True),
        inv_cov,
        precision=lax.Precision.HIGHEST,
        preferred_element_type=jnp.float32,
    )
    station_xy = jnp.take(site_xy, station_local, axis=1)
    block_width = math.gcd(site_block, 256)
    summed = lax.psum(partial_w, "site")
    weights = lax.all_to_all(
        summed.astype(jnp.bfloat16), "real", split_axis=0, concat_axis=1, tiled=True
    )
    piece = lax.all_gather(station_xy, "site", axis=1, tiled=True)

    def one_block(index, acc):
        anchor = index * block_width
        east = lax.dynamic_slice_in_dim(site_xy[0], anchor, block_width)
        north = lax.dynamic_slice_in_dim(site_xy[1], anchor, block_width)
        dist = jnp.sqrt(
            (east[:, None] - piece[0][None, :]) ** 2 + (north[:, None] - piece[1][None, :]) ** 2
        )
        cross = jnp.exp(-dist / 30.0).astype(jnp.bfloat16)
        term = lax.dot_general(
            weights, cross, (((1,), (1,)), ((), ())), preferred_element_type=jnp.float32
        )
        current = lax.dynamic_slice_in_dim(acc, anchor, block_width, 1)
        return lax.dynamic_update_slice_in_dim(acc, current + term, anchor, 1)

    cond_field = lax.fori_loop(0, site_block // block_width, one_block, field)
    ln_im = site_mean[None, :] + 0.6 * cond_field
    build_local = building_site - first_site
    build_im = jnp.take(ln_im, build_local, axis=1)
    class_count = median_ln.shape[1]
    class_table = (
        building_class[:, None] == jnp.arange(class_count, dtype=jnp.int32)[None, :]
    ).astype(jnp.float32)
    median_b = jnp.dot(
        median_ln,
        class_table.T,
        precision=lax.Precision.HIGHEST,
        preferred_element_type=jnp.float32,
    )
    step_b = jnp.dot(
        loss_step,
        class_table.T,
        precision=lax.Precision.HIGHEST,
        preferred_element_type=jnp.float32,
    )
    beta_b = jnp.dot(
        beta_ln[None, :],
        class_table.T,
        precision=lax.Precision.HIGHEST,
        preferred_element_type=jnp.float32,
    )
    exceed = normal_cdf((build_im[None, :, :] - median_b[:, None, :]) / beta_b[:, None, :])
    loss = building_value[None, :] * jnp.sum(exceed * step_b[:, None, :], axis=0)
    build_count = loss.shape[1]
    tract_count = TRACT_DEV * site_count
    group_width = math.gcd(build_count, 512)
    groups = build_count // group_width
    loss_groups = loss.reshape(real_rows, groups, group_width).transpose(1, 0, 2)
    tract_groups = building_tract.reshape(groups, group_width)

    def add_group(acc, pair):
        loss_part, tracts = pair
        table = (tracts[:, None] == jnp.arange(tract_count, dtype=jnp.int32)[None, :]).astype(
            jnp.float32
        )
        return (
            acc
            + jnp.dot(
                loss_part,
                table,
                precision=lax.Precision.HIGHEST,
                preferred_element_type=jnp.float32,
            ),
            None,
        )

    tract_part, _ = lax.scan(
        add_group, jnp.zeros((real_rows, tract_count), jnp.float32), (loss_groups, tract_groups)
    )
    all_buildings = build_count * site_count
    tract_loss = lax.psum_scatter(tract_part, "site", scatter_dimension=1, tiled=True)
    total_loss = lax.psum(jnp.sum(tract_loss, axis=1), "site") / all_buildings
    return (cond_field, tract_loss, total_loss)


def solution(mesh):
    placed = (
        P("real", "site"),
        P("site"),
        P("site", "real"),
        P(None, "site"),
        P("site"),
        P("site"),
        P("site"),
        P("site"),
        P("site"),
        P("site"),
        P(),
        P(),
        P(),
    )
    return jax.shard_map(
        shards,
        mesh=mesh,
        in_specs=placed,
        out_specs=(P("real", "site"), P("real", "site"), P("real")),
        check_vma=False,
    )
```

profile of v0, /device:TPU:0, one launch (start us, length us, event | category | flops | bytes accessed | tf_op | source)
XLA Modules:
  0.0 375.8 jit_solution(16030790064351147388)
XLA Ops:
  9.2 4.2 %gather_fusion.1 = f32[2560,16]{1,0:T(8,128)S(1)} fusion(f32[16,2048]{0,1:T(8,128)S(1)} %copy.54, s32[3072]{0:T(1024)S(1)} %pad_clamp_fusion), kind=kCustom, calls=%fused_computation.1 | custom fusion | bytes 337920 | tf_op jit(solution)/shard_map/jit(_take)/gather | solution.py:35
  13.3 1.8 subtract_bitcast_fusion
  15.5 19.6 %all_gather.7 = f32[64,2560]{1,0:T(8,128)S(1)} all-gather(f32[16,2560]{1,0:T(8,128)S(1)} %copy.55), channel_id=1, replica_groups=mesh['site'=8,'real'=4] {'real'}, dimensions={0}, use_global_device_ids=true | all-gather | bytes 819200 | tf_op jit(solution)/shard_map/all_gather | solution.py:38
  35.1 36.4 %fusion.17 = f32[64,5120]{1,0:T(8,128)S(1)} fusion(f32[64,2560]{1,0:T(8,128)S(1)} %all_gather.7, f32[2560,5120]{1,0:T(8,128)} %param.19), kind=kOutput, calls=%fused_computation.42 | convolution fusion | flops 10066329600 | bytes 54394880 | tf_op jit(solution)/shard_map/dot_general | solution.py:37
  71.6 51.7 %all-reduce.1 = bf16[64,5120]{1,0:T(8,128)(2,1)} all-reduce(f32[64,5120]{1,0:T(8,128)S(1)} %fusion.17), channel_id=1, replica_groups=mesh['site'=8,'real'=4] {'site'}, use_global_device_ids=true, to_apply=%region_0.1 | all-reduce | flops 327680 | bytes 1966080 | tf_op jit(solution)/shard_map/psum | solution.py:45
  123.2 3.8 all-to-all-start
  127.4 4.2 %gather_fusion = f32[2560,2]{1,0:T(8,128)S(1)} fusion(f32[2,2048]{0,1:T(8,128)S(1)} %copy.53, s32[3072]{0:T(1024)S(1)} %pad_clamp_fusion), kind=kCustom, calls=%fused_computation | custom fusion | bytes 51200 | tf_op jit(solution)/shard_map/jit(_take)/gather | solution.py:43
  131.5 1.4 select_bitcast_fusion.1
  132.9 51.0 %all_gather.6 = f32[2,20480]{0,1:T(8,128)} all-gather(f32[2,2560]{0,1:T(8,128)S(1)} %select_bitcast_fusion.1), channel_id=1, replica_groups=mesh['site'=8,'real'=4] {'site'}, dimensions={1}, use_global_device_ids=true | all-gather | bytes 184320 | tf_op jit(solution)/shard_map/all_gather | solution.py:49
  183.9 6.0 %copy.57 = f32[2,20480]{1,0:T(2,128)S(1)} copy(f32[2,20480]{0,1:T(8,128)} %all_gather.6) | data formatting | bytes 327680 | tf_op jit(solution)/shard_map/while | solution.py:65
  191.1 87.1 %while.24 = (s32[]{:T(128)}, f32[16,2048]{1,0:T(8,128)S(1)}, f32[2,2048]{1,0:T(2,128)S(1)}, f32[2,20480]{1,0:T(2,128)S(1)}, bf16[16,20480]{1,0:T(8,128)(2,1)S(1)...) while((s32[]{:T(128)}, f32[16,2048]{1,0:T(8,128)S(1)}, f32[2,2048]{1,0:T(2,128)S(1)}, ...), condition=%wide.region_2.3_spmd, body=%wide.region_1.2_spmd.sunk | while | flops 209719296 | bytes 1218715 | solution.py:65
  191.5 10.7 %fusion.31 = f32[16,2048]{1,0:T(8,128)S(1)} fusion(f32[16,2048]{1,0:T(8,128)S(1)} %get-tuple-element.281, s32[]{:T(128)S(6)} %select_n.57, bf16[16,20480]{1,0:T(8,128)(2,1)S(1)} %get-tuple-element.293, f32[20480]{0:T(1024)S(1)} %bitcast.59, f32[256]{0:T(256)S(1)} %bitcast.64, f32[20480]{0:T(1024)S(1)} %bitcast.58, f32[256]{0:T(256)S(1)} %bitcast.65), kind=kOutput, calls=%fused_computation.7.clone.1 | convolution fusion | flops 209719296 | bytes 854020 | tf_op jit(solution)/shard_map/while/body/eval_jaxpr/dot_general | solution.py:59
  202.4 10.7 %fusion.31 = f32[16,2048]{1,0:T(8,128)S(1)} fusion(f32[16,2048]{1,0:T(8,128)S(1)} %get-tuple-element.281, s32[]{:T(128)S(6)} %select_n.57, bf16[16,20480]{1,0:T(8,128)(2,1)S(1)} %get-tuple-element.293, f32[20480]{0:T(1024)S(1)} %bitcast.59, f32[256]{0:T(256)S(1)} %bitcast.64, f32[20480]{0:T(1024)S(1)} %bitcast.58, f32[256]{0:T(256)S(1)} %bitcast.65), kind=kOutput, calls=%fused_computation.7.clone.1 | convolution fusion | flops 209719296 | bytes 854020 | tf_op jit(solution)/shard_map/while/body/eval_jaxpr/dot_general | solution.py:59
  213.2 10.7 %fusion.31 = f32[16,2048]{1,0:T(8,128)S(1)} fusion(f32[16,2048]{1,0:T(8,128)S(1)} %get-tuple-element.281, s32[]{:T(128)S(6)} %select_n.57, bf16[16,20480]{1,0:T(8,128)(2,1)S(1)} %get-tuple-element.293, f32[20480]{0:T(1024)S(1)} %bitcast.59, f32[256]{0:T(256)S(1)} %bitcast.64, f32[20480]{0:T(1024)S(1)} %bitcast.58, f32[256]{0:T(256)S(1)} %bitcast.65), kind=kOutput, calls=%fused_computation.7.clone.1 | convolution fusion | flops 209719296 | bytes 854020 | tf_op jit(solution)/shard_map/while/body/eval_jaxpr/dot_general | solution.py:59
  224.1 10.7 %fusion.31 = f32[16,2048]{1,0:T(8,128)S(1)} fusion(f32[16,2048]{1,0:T(8,128)S(1)} %get-tuple-element.281, s32[]{:T(128)S(6)} %select_n.57, bf16[16,20480]{1,0:T(8,128)(2,1)S(1)} %get-tuple-element.293, f32[20480]{0:T(1024)S(1)} %bitcast.59, f32[256]{0:T(256)S(1)} %bitcast.64, f32[20480]{0:T(1024)S(1)} %bitcast.58, f32[256]{0:T(256)S(1)} %bitcast.65), kind=kOutput, calls=%fused_computation.7.clone.1 | convolution fusion | flops 209719296 | bytes 854020 | tf_op jit(solution)/shard_map/while/body/eval_jaxpr/dot_general | solution.py:59
  234.9 10.7 %fusion.31 = f32[16,2048]{1,0:T(8,128)S(1)} fusion(f32[16,2048]{1,0:T(8,128)S(1)} %get-tuple-element.281, s32[]{:T(128)S(6)} %select_n.57, bf16[16,20480]{1,0:T(8,128)(2,1)S(1)} %get-tuple-element.293, f32[20480]{0:T(1024)S(1)} %bitcast.59, f32[256]{0:T(256)S(1)} %bitcast.64, f32[20480]{0:T(1024)S(1)} %bitcast.58, f32[256]{0:T(256)S(1)} %bitcast.65), kind=kOutput, calls=%fused_computation.7.clone.1 | convolution fusion | flops 209719296 | bytes 854020 | tf_op jit(solution)/shard_map/while/body/eval_jaxpr/dot_general | solution.py:59
  245.8 10.7 %fusion.31 = f32[16,2048]{1,0:T(8,128)S(1)} fusion(f32[16,2048]{1,0:T(8,128)S(1)} %get-tuple-element.281, s32[]{:T(128)S(6)} %select_n.57, bf16[16,20480]{1,0:T(8,128)(2,1)S(1)} %get-tuple-element.293, f32[20480]{0:T(1024)S(1)} %bitcast.59, f32[256]{0:T(256)S(1)} %bitcast.64, f32[20480]{0:T(1024)S(1)} %bitcast.58, f32[256]{0:T(256)S(1)} %bitcast.65), kind=kOutput, calls=%fused_computation.7.clone.1 | convolution fusion | flops 209719296 | bytes 854020 | tf_op jit(solution)/shard_map/while/body/eval_jaxpr/dot_general | solution.py:59
  256.7 10.7 %fusion.31 = f32[16,2048]{1,0:T(8,128)S(1)} fusion(f32[16,2048]{1,0:T(8,128)S(1)} %get-tuple-element.281, s32[]{:T(128)S(6)} %select_n.57, bf16[16,20480]{1,0:T(8,128)(2,1)S(1)} %get-tuple-element.293, f32[20480]{0:T(1024)S(1)} %bitcast.59, f32[256]{0:T(256)S(1)} %bitcast.64, f32[20480]{0:T(1024)S(1)} %bitcast.58, f32[256]{0:T(256)S(1)} %bitcast.65), kind=kOutput, calls=%fused_computation.7.clone.1 | convolution fusion | flops 209719296 | bytes 854020 | tf_op jit(solution)/shard_map/while/body/eval_jaxpr/dot_general | solution.py:59
  267.5 10.7 %fusion.31 = f32[16,2048]{1,0:T(8,128)S(1)} fusion(f32[16,2048]{1,0:T(8,128)S(1)} %get-tuple-element.281, s32[]{:T(128)S(6)} %select_n.57, bf16[16,20480]{1,0:T(8,128)(2,1)S(1)} %get-tuple-element.293, f32[20480]{0:T(1024)S(1)} %bitcast.59, f32[256]{0:T(256)S(1)} %bitcast.64, f32[20480]{0:T(1024)S(1)} %bitcast.58, f32[256]{0:T(256)S(1)} %bitcast.65), kind=kOutput, calls=%fused_computation.7.clone.1 | convolution fusion | flops 209719296 | bytes 854020 | tf_op jit(solution)/shard_map/while/body/eval_jaxpr/dot_general | solution.py:59
  278.6 14.1 %gather_fusion.2 = f32[4096,16]{1,0:T(8,128)} fusion(f32[16,2048]{0,1:T(8,128)S(1)} %copy.58, s32[4096]{0:T(1024)S(1)} %fusion.13), kind=kCustom, calls=%fused_computation.2 | custom fusion | bytes 540672 | tf_op jit(solution)/shard_map/jit(_take)/gather | solution.py:68
  292.7 3.6 select_bitcast_fusion
  297.4 22.7 %while.25 = (s32[]{:T(128)}, f32[16,4096]{1,0:T(8,128)S(1)}, f32[8,16,512]{2,0,1:T(8,128)S(1)}, s32[8,512]{1,0:T(8,128)S(1)}, s32[]{:T(128)}, /*index=5*/s32[]{:T(128)}) while((s32[]{:T(128)}, f32[16,4096]{1,0:T(8,128)S(1)}, f32[8,16,512]{2,0,1:T(8,128)S(1)}, s32[8,512]{1,0:T(8,128)S(1)}, s32[]{:T(128)}, /*index=5*/s32[]{:T(128)}) %tuple.76), condition=%wide.region_5.6_spmd.clone, body=%wide.region_4.5_spmd.clone.sunk | while | flops 404881408 | bytes 628831 | solution.py:116
  297.4 2.8 fusion.32
  300.3 2.8 fusion.32
  303.1 2.8 fusion.32
  305.9 2.8 fusion.32
  308.8 2.8 fusion.32
  311.6 2.8 fusion.32
  314.4 2.8 fusion.32
  317.3 2.8 fusion.32
  320.8 34.5 %reduce-scatter.2.cloned.1.call-done = f32[16,512]{1,0:T(8,128)} async-done(((f32[16,4096]{1,0:T(8,128)}), f32[16,512]{1,0:T(8,128)}) %reduce-scatter.2.cloned.1.call-update) | async-done | bytes 32784 | tf_op jit(solution)/shard_map/reduce_scatter | solution.py:120
  356.2 12.2 %psum.15 = f32[16]{0:T(128)S(1)} all-reduce(f32[16]{0:T(128)S(1)} %reduce_sum.22), channel_id=1, replica_groups=mesh['site'=8,'real'=4] {'site'}, use_global_device_ids=true, to_apply=%region_8.9 | all-reduce | flops 16 | bytes 128 | tf_op jit(solution)/shard_map/psum | solution.py:121
  (92 shorter events, 8.8 us)
Async XLA Ops:
  7.2 183.2 %copy-start = (f32[4,36]{1,0:T(4,128)S(1)}, f32[4,36]{1,0:T(4,128)}, u32[]{:S(2)}) copy-start(f32[4,36]{1,0:T(4,128)} %param.29) | copy-start | bytes 1732
  7.2 6.1 %copy-start.8 = (f32[2560]{0:T(1024)S(1)}, f32[2560]{0:T(1024)}, u32[]{:S(2)}) copy-start(f32[2560]{0:T(1024)} %param.18) | copy-start | bytes 30724
  71.6 55.4 %copy-start.3 = (f32[2,2048]{1,0:T(2,128)S(1)}, f32[2,2048]{1,0:T(2,128)}, u32[]{:S(2)}) copy-start(f32[2,2048]{1,0:T(2,128)} %param.20) | copy-start | bytes 49156
  123.2 67.8 %all-to-all-start = ((bf16[4,16,5120]{2,1,0:T(8,128)(2,1)}), bf16[4,16,5120]{2,1,0:T(8,128)(2,1)S(1)}, u32[]{:S(2)}, u32[]{:S(2)}) async-start(bf16[4,16,5120]{2,1,0:T(8,128)(2,1)} %bitcast.7), calls=%async_computation | async-start | bytes 1310720 | tf_op jit(solution)/shard_map/all_to_all | solution.py:46
  127.0 5.9 %copy-start.5 = (s32[4096]{0:T(1024)S(1)}, s32[4096]{0:T(1024)}, u32[]{:S(2)}) copy-start(s32[4096]{0:T(1024)} %param.23) | copy-start | bytes 49156
  127.0 228.3 %reduce-scatter.2.cloned.1.call-start = ((), (), s32[]{:S(2)}) async-start(), calls=%async_computation.2 | async-start | bytes 294912 | tf_op jit(solution)/shard_map/reduce_scatter | solution.py:120
  183.9 6.1 %copy-start.6 = (f32[4096]{0:T(1024)S(1)}, f32[4096]{0:T(1024)}, u32[]{:S(2)}) copy-start(f32[4096]{0:T(1024)} %param.26) | copy-start | bytes 49156
  183.9 6.1 %copy-start.7 = (s32[4096]{0:T(1024)S(1)}, s32[4096]{0:T(1024)}, u32[]{:S(2)}) copy-start(s32[4096]{0:T(1024)} %param.25) | copy-start | bytes 49156
  183.9 6.1 %copy-start.10 = (s32[4096]{0:T(1024)S(1)}, s32[4096]{0:T(1024)}, u32[]{:S(2)}) copy-start(s32[4096]{0:T(1024)} %param.24) | copy-start | bytes 49156
  183.9 6.1 %copy-start.12 = (f32[36]{0:T(128)S(1)}, f32[36]{0:T(128)}, u32[]{:S(2)}) copy-start(f32[36]{0:T(128)} %param.28) | copy-start | bytes 436
  183.9 6.8 %copy-start.11 = (f32[4,36]{1,0:T(4,128)S(1)}, f32[4,36]{1,0:T(4,128)}, u32[]{:S(2)}) copy-start(f32[4,36]{1,0:T(4,128)} %param.27) | copy-start | bytes 1732
  191.1 87.1 %copy-start.9 = (f32[2048]{0:T(1024)S(1)}, f32[2048]{0:T(1024)}, u32[]{:S(2)}) copy-start(f32[2048]{0:T(1024)} %param.22) | copy-start | bytes 24580
  278.2 18.1 %copy-start.2 = (f32[16,2048]{1,0:T(8,128)}, f32[16,2048]{1,0:T(8,128)S(1)}, u32[]{:S(2)}) copy-start(f32[16,2048]{1,0:T(8,128)S(1)} %get-tuple-element.116) | copy-start | bytes 393220
  320.1 0.7 copy-start.4
  320.1 48.9 %copy-start.1 = (f32[4,36]{1,0:T(4,128)S(1)}, f32[4,36]{1,0:T(4,128)}, u32[]{:S(2)}) copy-start(f32[4,36]{1,0:T(4,128)} %param.29) | copy-start | bytes 1732
Sparse Core Ops, SparseCore 0:
  320.9 34.3 reduce-scatter.1
where the time goes:
time: 376 us
  matrix products  145 us (39%)
  blocking collectives  134 us (36%)
  waiting for transfers between devices  34.5 us (9%)
  local copies, waits for them, and re-layouts  33.8 us (9%)
  between operations  14.3 us (4%)
  other arithmetic  9.19 us (2%)
    dot_general x8, matrix products, one_block(): lax.dot_general(weights, cross, (((1,), (1,)), ((), ())), preferred_eleme...  85.4 us
    psum x1, blocking collectives, shards(): summed = lax.psum(partial_w, 'site')  51.7 us
    all_gather x1, blocking collectives, shards(): piece = lax.all_gather(station_xy, 'site', axis=1, tiled=True)  51 us
    dot_general x1, matrix products, shards(): jnp.dot(lax.all_gather(innov, 'real', axis=0, tiled=True), inv_cov, preci...  36.4 us
    reduce_scatter x1, waiting for transfers between devices, shards(): lax.psum_scatter(tract_part, 'site', scatter_dimension=1, tiled=True)  34.5 us
    dot_general x8, matrix products, add_group(): jnp.dot(loss_part, table, precision=lax.Precision.HIGHEST, preferred_elem...  22.2 us
    all_gather x1, blocking collectives, shards(): lax.all_gather(innov, 'real', axis=0, tiled=True)  19.6 us
    gather x1, local copies, waits for them, and re-layouts, shards(): build_im = jnp.take(ln_im, build_local, axis=1)  14.1 us
  transfers between devices with their start and end apart: 2, of which 1 were waited for; matrix products, arithmetic and copies ran while one was open for 3% of the time, Pallas kernels for 0%

commit v1 on v0

v1 whole, which is shorter than its diff:
```python
import functools
import math

import jax
import jax.numpy as jnp
from jax import lax
from jax.experimental import pallas as pl
from jax.experimental.pallas import tpu as pltpu
from jax.sharding import PartitionSpec as P

MESH = pl.DeviceIdType.MESH
F32 = jnp.float32
BF16 = jnp.bfloat16
COORD_SCALE = math.log2(math.e) / 30.0
TRACT_DEV = 512


def split2(x):
    hi = x.astype(BF16).astype(F32)
    return hi, x - hi


def split3(x):
    hi, rest = split2(x)
    mid, low = split2(rest)
    return hi, mid, low


def onehot_gather(table_ref, index_ref, width, block, store):
    count = index_ref.shape[1]
    sites = table_ref.shape[1]

    def chunk(n, carry):
        start = pl.multiple_of(n * width, 128)
        index = index_ref[:, pl.ds(start, width)]
        total = jnp.zeros((table_ref.shape[0], width), F32)
        for s in range(sites // block):
            rows = lax.broadcasted_iota(jnp.int32, (block, width), 0) + s * block
            hot = jnp.where(rows == index, 1.0, 0.0).astype(BF16)
            total += jnp.dot(
                table_ref[:, s * block : (s + 1) * block], hot, preferred_element_type=F32
            )
        store(start, total)
        return carry

    lax.fori_loop(0, count // width, chunk, 0)


def krige_kernel(
    n_site,
    n_real,
    groups,
    steps,
    nbuf,
    field_ref,
    observed_ref,
    inv_ref,
    xy_ref,
    local_ref,
    cond_ref,
    table,
    innov_all,
    xy_rows,
    xy_col,
    tiles,
    cross,
    part,
    got,
    wout,
    acc,
    back,
    back_in,
    tile_sem,
    i_send,
    i_recv,
    x_send,
    x_recv,
    p_send,
    p_recv,
    w_send,
    w_recv,
    b_send,
    b_recv,
):
    me_s = lax.axis_index("site")
    me_r = lax.axis_index("real")
    rr, sites = field_ref.shape
    ns = observed_ref.shape[1]
    reals = n_real * rr
    per = n_site // n_real
    tw = tiles.shape[2]
    gw = tw * steps
    rows_o = reals // n_site
    k = 16 // rows_o
    mw = gw // k
    total_steps = groups * steps

    barrier = pltpu.get_barrier_semaphore()
    for j in range(1, n_site):
        pl.semaphore_signal(
            barrier, inc=1, device_id=(lax.rem(me_s + j, n_site), me_r), device_id_type=MESH
        )
    for j in range(1, n_real):
        pl.semaphore_signal(
            barrier, inc=1, device_id=(me_s, lax.rem(me_r + j, n_real)), device_id_type=MESH
        )

    def tile_copy(c):
        slot = lax.rem(c, nbuf)
        col = pl.multiple_of(c * tw, 128)
        return pltpu.make_async_copy(
            inv_ref.at[:, pl.ds(col, tw)], tiles.at[slot], tile_sem.at[slot]
        )

    for c in range(nbuf):
        tile_copy(c).start()

    fh, fl = split2(field_ref[...])
    xa, xb, xc = split3(xy_ref[...] * COORD_SCALE)
    table[...] = jnp.concatenate(
        [fh, fl, xa, xb, xc, jnp.zeros((10, sites), F32)], axis=0
    ).astype(BF16)

    me_slot = lax.rem(me_s, per)
    mine = me_s // per == me_r

    def store(start, got_rows):
        width = got_rows.shape[1]
        station = got_rows[:rr] + got_rows[rr : 2 * rr]
        xys = (
            got_rows[2 * rr : 2 * rr + 2]
            + got_rows[2 * rr + 2 : 2 * rr + 4]
            + got_rows[2 * rr + 4 : 2 * rr + 6]
        )
        innov = observed_ref[:, pl.ds(start, width)] - station
        hi, low = split2(innov)
        innov_all[me_r, :, pl.ds(start, width)] = jnp.concatenate([hi, low], axis=0).astype(BF16)
        xy_rows[per, :, pl.ds(start, width)] = jnp.concatenate(
            [xys, jnp.zeros((6, width), F32)], axis=0
        )

    onehot_gather(table, local_ref, math.gcd(ns, 512), 256, store)

    pl.semaphore_wait(barrier, n_site - 1 + n_real - 1)

    def innov_copy(j):
        return pltpu.make_async_remote_copy(
            src_ref=innov_all.at[me_r],
            dst_ref=innov_all.at[me_r],
            send_sem=i_send.at[j],
            recv_sem=i_recv.at[j],
            device_id=(me_s, lax.rem(me_r + j, n_real)),
            device_id_type=MESH,
        )

    def xy_copy(j):
        return pltpu.make_async_remote_copy(
            src_ref=xy_rows.at[per],
            dst_ref=xy_rows.at[me_slot],
            send_sem=x_send.at[j],
            recv_sem=x_recv.at[me_slot],
            device_id=(lax.rem(me_s + j, n_site), me_r),
            device_id_type=MESH,
        )

    @pl.when(mine)
    def _():
        for j in range(1, n_site):
            xy_copy(j).start()

    for j in range(1, n_real):
        innov_copy(j).start()

    @pl.when(mine)
    def _():
        xy_rows[me_slot] = xy_rows[per]

    for s in range(per):

        @pl.when(jnp.logical_not(jnp.logical_and(mine, me_slot == s)))
        def _():
            pltpu.make_async_remote_copy(
                src_ref=xy_rows.at[per],
                dst_ref=xy_rows.at[s],
                send_sem=x_send.at[0],
                recv_sem=x_recv.at[s],
                device_id=(lax.rem(me_s + 1, n_site), me_r),
                device_id_type=MESH,
            ).wait_recv()

    for s in range(per):
        xy_col[s * ns : (s + 1) * ns, :] = xy_rows[s].T

    for j in range(1, n_real):
        innov_copy(j).wait_recv()

    east = xy_ref[0:1, :] * COORD_SCALE
    north = xy_ref[1:2, :] * COORD_SCALE
    kt = math.gcd(ns, 256)
    k_count = ns // kt
    pieces = tw // 16
    acc[...] = jnp.zeros_like(acc)

    def part_copy(g, j):
        peer = lax.rem(me_s + j, n_site)
        return pltpu.make_async_remote_copy(
            src_ref=part.at[g, peer],
            dst_ref=got.at[g, me_s],
            send_sem=p_send.at[g, j],
            recv_sem=p_recv.at[g, j],
            device_id=(peer, me_r),
            device_id_type=MESH,
        )

    def w_copy(g, j):
        peer = lax.rem(me_s + j, n_site)
        return pltpu.make_async_remote_copy(
            src_ref=wout.at[g, me_s],
            dst_ref=wout.at[g, me_s],
            send_sem=w_send.at[g, j],
            recv_sem=w_recv.at[g, j],
            device_id=(peer, me_r),
            device_id_type=MESH,
        )

    def sum_and_share(g):
        for j in range(1, n_site):
            part_copy(g, j).wait_recv()
        got[g, me_s] = part[g, me_s]
        total = got[g, 0]
        for s in range(1, n_site):
            total += got[g, s]
        wout[g, me_s] = jnp.concatenate(
            [total[:, i * mw : (i + 1) * mw] for i in range(k)], axis=0
        ).astype(BF16)
        for j in range(1, n_site):
            w_copy(g, j).start()

    def apply_group(g, width, after):
        for j in range(1, n_site):
            w_copy(g, j).wait_recv()
        weights = wout[g].astype(F32)
        weights = jnp.concatenate(
            [
                jnp.concatenate(
                    [weights[s, i * rows_o : (i + 1) * rows_o] for i in range(k)], axis=1
                )
                for s in range(n_site)
            ],
            axis=0,
        ).astype(BF16)
        row = pl.multiple_of(g * gw, 128)
        for n in range(sites // width):
            cols = slice(n * width, (n + 1) * width)
            acc[:, cols] += jnp.dot(
                weights, cross[pl.ds(row, gw), cols], preferred_element_type=F32
            )
            after(n)

    def one_step(q, g):
        c = g * steps + q
        slot = lax.rem(c, nbuf)
        tile_copy(c).wait()
        lhs = innov_all[...].reshape(n_real * 2 * rr, ns)
        product = jnp.zeros((n_real * 2 * rr, tw), F32)
        done = 0
        for p in range(k_count):
            product += jnp.dot(
                lhs[:, p * kt : (p + 1) * kt],
                tiles[slot, p * kt : (p + 1) * kt, :].astype(BF16),
                preferred_element_type=F32,
            )
            upto = (p + 1) * pieces // k_count
            for m in range(done, upto):
                row = pl.multiple_of(c * tw + m * 16, 16)
                dx = xy_col[pl.ds(row, 16), 0:1] - east
                dy = xy_col[pl.ds(row, 16), 1:2] - north
                d2 = jnp.maximum(dx * dx + dy * dy, 1e-20)
                cross[pl.ds(row, 16), :] = jnp.exp2(-(d2 * lax.rsqrt(d2))).astype(BF16)
            done = upto
        product = product.reshape(n_real, 2, rr, tw)
        partial = (product[:, 0] + product[:, 1]).reshape(n_site, rows_o, tw)
        part[g, :, :, pl.ds(pl.multiple_of(q * tw, 128), tw)] = partial

        @pl.when(c + nbuf < total_steps)
        def _():
            tile_copy(c + nbuf).start()

        return g

    def one_group(g, carry):
        lax.fori_loop(0, steps, one_step, g)
        for j in range(1, n_site):
            part_copy(g, j).start()

        @pl.when(g >= 1)
        def _():
            sum_and_share(g - 1)

        @pl.when(g >= 2)
        def _():
            apply_group(g - 2, 512, lambda n: None)

        return carry

    lax.fori_loop(0, groups, one_group, 0)

    def back_copy(j, n):
        peer = lax.rem(me_r + j, n_real)
        return pltpu.make_async_remote_copy(
            src_ref=back.at[n, peer],
            dst_ref=back_in.at[n, me_r],
            send_sem=b_send.at[n, j],
            recv_sem=b_recv.at[n, j],
            device_id=(me_s, peer),
            device_id_type=MESH,
        )

    bw = back.shape[3] * (back.shape[2] // rr)
    kb = bw // back.shape[3]

    def send_back(n):
        for z in range(n_real):
            block = acc[z * rr : (z + 1) * rr, n * bw : (n + 1) * bw]
            w = bw // kb
            back[n, z] = jnp.concatenate(
                [block[:, i * w : (i + 1) * w] for i in range(kb)], axis=0
            ).astype(BF16)
        for j in range(1, n_real):
            back_copy(j, n).start()

    apply_group(groups - 2, 512, lambda n: None)
    sum_and_share(groups - 1)
    apply_group(groups - 1, bw, send_back)

    own_row = pl.multiple_of(me_r * rr, 8)
    for n in range(sites // bw):
        for j in range(1, n_real):
            back_copy(j, n).wait_recv()
        back_in[n, me_r] = jnp.zeros_like(back_in[n, 0])
        total = back_in[n, 0].astype(F32)
        for z in range(1, n_real):
            total += back_in[n, z].astype(F32)
        total = jnp.concatenate([total[i * rr : (i + 1) * rr] for i in range(kb)], axis=1)
        cols = slice(n * bw, (n + 1) * bw)
        cond_ref[:, cols] = field_ref[:, cols] + acc[pl.ds(own_row, rr), cols] + total

    for j in range(1, n_real):
        innov_copy(j).wait_send()
        for n in range(sites // bw):
            back_copy(j, n).wait_send()

    @pl.when(mine)
    def _():
        for j in range(1, n_site):
            xy_copy(j).wait_send()

    def drain(g, carry):
        for j in range(1, n_site):
            part_copy(g, j).wait_send()
            w_copy(g, j).wait_send()
        return carry

    lax.fori_loop(0, groups, drain, 0)


def loss_kernel(
    n_site,
    all_buildings,
    cond_ref,
    mean_ref,
    local_ref,
    class_ref,
    tract_ref,
    value_ref,
    params_ref,
    out_ref,
    sum_ref,
    table,
    loss_ref,
    lo_hot,
    send,
    recv,
    s_sem,
    r_sem,
):
    me_s = lax.axis_index("site")
    me_r = lax.axis_index("real")
    rr = cond_ref.shape[0]
    count = local_ref.shape[1]
    barrier = pltpu.get_barrier_semaphore()
    for j in range(1, n_site):
        pl.semaphore_signal(
            barrier, inc=1, device_id=(lax.rem(me_s + j, n_site), me_r), device_id_type=MESH
        )
    hi, low = split2(mean_ref[...] + 0.6 * cond_ref[...])
    table[...] = jnp.concatenate([hi, low], axis=0).astype(BF16)
    classes = params_ref.shape[1]

    def store(start, rows):
        width = rows.shape[1]
        here = pl.ds(start, width)
        im = rows[:rr] + rows[rr:]
        hot = jnp.where(
            lax.broadcasted_iota(jnp.int32, (classes, width), 0) == class_ref[:, here], 1.0, 0.0
        )
        par = jnp.dot(
            params_ref[...], hot, precision=lax.Precision.HIGHEST, preferred_element_type=F32
        )
        inverse = 0.7071067811865476 / par[4:5]
        total = jnp.zeros((rr, width), F32)
        for s in range(4):
            v = (im - par[s : s + 1]) * inverse
            total += (0.5 * (1.0 + lax.erf(v))) * par[8 + s : 9 + s]
        loss = value_ref[:, here] * total
        a, b = split2(loss)
        loss_ref[:, here] = jnp.concatenate([a, b], axis=0)
        tract_low = lax.rem(tract_ref[:, here], 128)
        lo_hot[:, here] = jnp.where(
            lax.broadcasted_iota(jnp.int32, (128, width), 0) == tract_low, 1.0, 0.0
        ).astype(BF16)

    onehot_gather(table, local_ref, math.gcd(count, 512), 256, store)

    local_total = jnp.sum(loss_ref[:rr] + loss_ref[rr:], axis=1, keepdims=True)
    local_total = jnp.broadcast_to(local_total, (rr, 128))
    per_dev = TRACT_DEV // 128
    tract_high = tract_ref[...] // 128

    def one_owner(d, carry):
        left = jnp.concatenate(
            [
                jnp.where(tract_high == d * per_dev + h, loss_ref[...], 0.0).astype(BF16)
                for h in range(per_dev)
            ],
            axis=0,
        )
        sums = lax.dot_general(
            left, lo_hot[...], (((1,), (1,)), ((), ())), preferred_element_type=F32
        )
        for h in range(per_dev):
            base = h * 2 * rr
            send[d, :, h * 128 : (h + 1) * 128] = (
                sums[base : base + rr] + sums[base + rr : base + 2 * rr]
            )
        send[d, :, TRACT_DEV:] = local_total
        return carry

    lax.fori_loop(0, n_site, one_owner, 0)
    pl.semaphore_wait(barrier, n_site - 1)

    def copy(j):
        peer = lax.rem(me_s + j, n_site)
        return pltpu.make_async_remote_copy(
            src_ref=send.at[peer],
            dst_ref=recv.at[me_s],
            send_sem=s_sem.at[j],
            recv_sem=r_sem.at[j],
            device_id=(peer, me_r),
            device_id_type=MESH,
        )

    for j in range(1, n_site):
        copy(j).start()
    recv[me_s] = send[me_s]
    for j in range(1, n_site):
        copy(j).wait_recv()
    total = recv[0]
    for s in range(1, n_site):
        total += recv[s]
    out_ref[...] = total[:, :TRACT_DEV]
    sum_ref[...] = total[:, TRACT_DEV:] / all_buildings
    for j in range(1, n_site):
        copy(j).wait_send()


def shards(
    n_site,
    n_real,
    field,
    observed,
    inv_cov,
    site_xy,
    station_site,
    site_mean,
    building_site,
    building_class,
    building_tract,
    building_value,
    median_ln,
    beta_ln,
    loss_step,
):
    rr, sites = field.shape
    ns, cols = inv_cov.shape
    first_site = lax.axis_index("site") * sites
    reals = rr * n_real
    per = n_site // n_real
    tw = 256
    groups = 5
    steps = cols // groups // tw
    nbuf = min(6, groups * steps)
    gw = tw * steps
    rows_o = reals // n_site
    k = 16 // rows_o
    bw = math.gcd(sites, 512)
    kb = max(1, 16 // rr)
    vmem = pl.BlockSpec(memory_space=pltpu.VMEM)
    dma = pltpu.SemaphoreType.DMA
    cond = pl.pallas_call(
        functools.partial(krige_kernel, n_site, n_real, groups, steps, nbuf),
        out_shape=jax.ShapeDtypeStruct((rr, sites), F32),
        in_specs=[vmem, vmem, pl.BlockSpec(memory_space=pl.ANY), vmem, vmem],
        out_specs=vmem,
        scratch_shapes=[
            pltpu.VMEM((2 * rr + 16, sites), BF16),
            pltpu.VMEM((n_real, 2 * rr, ns), BF16),
            pltpu.VMEM((per + 1, 8, ns), F32),
            pltpu.VMEM((cols, 8), F32),
            pltpu.VMEM((nbuf, ns, tw), F32),
            pltpu.VMEM((cols, sites), BF16),
            pltpu.VMEM((groups, n_site, rows_o, gw), F32),
            pltpu.VMEM((groups, n_site, rows_o, gw), F32),
            pltpu.VMEM((groups, n_site, 16, gw // k), BF16),
            pltpu.VMEM((reals, sites), F32),
            pltpu.VMEM((sites // bw, n_real, kb * rr, bw // kb), BF16),
            pltpu.VMEM((sites // bw, n_real, kb * rr, bw // kb), BF16),
            dma((nbuf,)),
            dma((n_real,)),
            dma((n_real,)),
            dma((n_site,)),
            dma((per,)),
            dma((groups, n_site)),
            dma((groups, n_site)),
            dma((groups, n_site)),
            dma((groups, n_site)),
            dma((sites // bw, n_real)),
            dma((sites // bw, n_real)),
        ],
        compiler_params=pltpu.CompilerParams(
            collective_id=0, has_side_effects=True, vmem_limit_bytes=56 * 2**20
        ),
    )(
        field,
        observed.reshape(1, ns),
        inv_cov,
        site_xy,
        (station_site - first_site).reshape(1, ns),
    )
    count = building_site.shape[0]
    classes = median_ln.shape[1]
    params = jnp.concatenate(
        [median_ln, beta_ln[None, :], jnp.ones((3, classes), F32), loss_step, jnp.ones((4, classes), F32)]
    )
    params = jnp.pad(params, ((0, 0), (0, 128 - classes)))
    tract, total = pl.pallas_call(
        functools.partial(loss_kernel, n_site, count * n_site),
        out_shape=(
            jax.ShapeDtypeStruct((rr, TRACT_DEV), F32),
            jax.ShapeDtypeStruct((rr, 128), F32),
        ),
        in_specs=[vmem] * 7,
        out_specs=(vmem, vmem),
        scratch_shapes=[
            pltpu.VMEM((2 * rr, sites), BF16),
            pltpu.VMEM((2 * rr, count), F32),
            pltpu.VMEM((128, count), BF16),
            pltpu.VMEM((n_site, rr, TRACT_DEV + 128), F32),
            pltpu.VMEM((n_site, rr, TRACT_DEV + 128), F32),
            dma((n_site,)),
            dma((n_site,)),
        ],
        compiler_params=pltpu.CompilerParams(
            collective_id=1, has_side_effects=True, vmem_limit_bytes=40 * 2**20
        ),
    )(
        cond,
        site_mean.reshape(1, sites),
        (building_site - first_site).reshape(1, count),
        building_class.reshape(1, count),
        building_tract.reshape(1, count),
        building_value.reshape(1, count),
        params,
    )
    return cond, tract, total[:, 0]


def solution(mesh):
    placed = (
        P("real", "site"),
        P("site"),
        P("site", "real"),
        P(None, "site"),
        P("site"),
        P("site"),
        P("site"),
        P("site"),
        P("site"),
        P("site"),
        P(),
        P(),
        P(),
    )
    return jax.shard_map(
        functools.partial(shards, mesh.shape["site"], mesh.shape["real"]),
        mesh=mesh,
        in_specs=placed,
        out_specs=(P("real", "site"), P("real", "site"), P("real")),
        check_vma=False,
    )
```

time: 376 us -> 87 us (0.23)
  matrix products: 145 us -> 0 us
  blocking collectives: 134 us -> 0 us
  Pallas kernels: 0 us -> 80.3 us
  waiting for transfers between devices: 34.5 us -> 0 us
  local copies, waits for them, and re-layouts: 33.8 us -> 4.8 us
  between operations: 14.3 us -> 0.81 us
  other arithmetic: 9.19 us -> 0.76 us
    dot_general x20 -> x0, matrix products: 145 us -> none  [the longest x8 85.4 us: one_block(): lax.dot_general(weights, cross, (((1,), (1,)), ((), ())), preferred_eleme...]
    pallas_call x0 -> x2, Pallas kernels: none -> 80.3 us  [the longest x1 66.2 us: shards(): pl.pallas_call(functools.partial(krige_kernel, n_site, n_real, groups, st...]
    all_gather x2 -> x0, blocking collectives: 70.6 us -> none  [the longest x1 51 us: shards(): piece = lax.all_gather(station_xy, 'site', axis=1, tiled=True)]
    psum x2 -> x0, blocking collectives: 63.9 us -> none  [the longest x1 51.7 us: shards(): summed = lax.psum(partial_w, 'site')]
    reduce_scatter x1 -> x0, waiting for transfers between devices: 34.5 us -> none  [shards(): lax.psum_scatter(tract_part, 'site', scatter_dimension=1, tiled=True)]
    gather x3 -> x0, local copies, waits for them, and re-layouts: 22.4 us -> none  [the longest x1 14.1 us: shards(): build_im = jnp.take(ln_im, build_local, axis=1)]
    while x1 -> x0, local copies, waits for them, and re-layouts: 6.04 us -> none  [shards(): cond_field = lax.fori_loop(0, site_block // block_width, one_block, field)]
    select_n x2 -> x0, other arithmetic: 4.96 us -> none  [the longest x1 3.61 us: shards(): build_im = jnp.take(ln_im, build_local, axis=1)]
  transfers between devices with their start and end apart: 2 -> 0, of which waited for: 1 -> 0; matrix products, arithmetic and copies ran while one was open for 3% -> 0% of each run, Pallas kernels for 0% -> 0%
where the time goes in v1:
time: 87 us; the launch traced here: 86.7 us
  Pallas kernels  80.3 us (92%)
  local copies, waits for them, and re-layouts  4.8 us (6%)
    pallas_call x1, Pallas kernels, shards(): pl.pallas_call(functools.partial(krige_kernel, n_site, n_real, groups, st...  66.2 us
    pallas_call x1, Pallas kernels, shards(): pl.pallas_call(functools.partial(loss_kernel, n_site, count * n_site), ou...  14.1 us
    unnamed x20, local copies, waits for them, and re-layouts  2.2 us

profile of v1, /device:TPU:0, one launch (start us, length us, event | category | flops | bytes accessed | tf_op | source)
XLA Modules:
  0.0 86.7 jit_solution(16495898132854112101)
XLA Ops:
  0.6 0.0 copy-start.5
  0.6 0.0 copy-start.8
  0.7 0.0 copy-start.6
  0.7 0.0 copy-start.7
  0.7 0.0 copy-start.4
  0.7 0.0 copy-start.1
  0.7 0.0 copy-start.2
  0.7 0.0 copy-start.3
  0.7 0.8 broadcast_subtract_fusion.1
  1.5 0.6 reshape.28.local_ref
  2.1 1.3 %reshape.27.observed_ref = f32[1,2560]{1,0:T(1,128)} reshape(f32[2560]{0:T(1024)} %param.14) | data formatting | bytes 20480 | tf_op jit(solution)/shard_map/reshape | solution.py:545
  3.4 66.2 %shard_map.148.cond_ref = f32[16,2048]{1,0:T(8,128)} custom-call(f32[16,2048]{1,0:T(8,128)} %field_ref.1, f32[1,2560]{1,0:T(1,128)} %reshape.27.observed_ref, f32[2560,5120]{1,0:T(8,128)} %inv_ref.1, f32[2,2048]{1,0:T(2,128)} %xy_ref.1, s32[1,2560]{1,0:T(1,128)} %reshape.28.local_ref), custom_call_target="tpu_custom_call" | custom-call | tf_op jit(solution)/shard_map/pallas_call | solution.py:510
  69.6 0.0 copy-done.5
  69.7 0.0 copy-done.8
  69.7 0.0 copy-done.6
  69.7 0.0 copy-done.7
  69.8 0.0 copy-done.4
  69.8 0.0 copy-done.1
  69.8 0.0 copy-done.2
  69.8 0.0 copy-done.3
  69.8 0.0 copy-start
  69.8 0.9 %copy-done = f32[16,2048]{1,0:T(8,128)S(1)} copy-done((f32[16,2048]{1,0:T(8,128)S(1)}, f32[16,2048]{1,0:T(8,128)}, u32[]{:S(2)}) %copy-start) | copy-done | bytes 131096
  70.7 14.1 %shard_map.149 = (f32[16,512]{1,0:T(8,128)S(1)}, f32[16,128]{1,0:T(8,128)S(1)}) custom-call(f32[16,2048]{1,0:T(8,128)S(1)} %copy-done, f32[1,2048]{1,0:T(1,128)S(1)} %bitcast.10, s32[1,4096]{1,0:T(1,128)S(1)} %bitcast.6, s32[1,4096]{1,0:T(1,128)S(1)} %bitcast.7, s32[1,4096]{1,0:T(1,128)S(1)} %bitcast.8, f32[1,4096]{1,0:T(1,128)S(1)} %bitcast.9, ...), custom_call_target="tpu_custom_call" | custom-call | tf_op jit(solution)/shard_map/pallas_call | solution.py:556
  84.8 0.6 slice_reduce_fusion
  85.4 0.7 copy.18
  86.1 0.6 copy.19
  (5 shorter events, 0.1 us)
Async XLA Ops:
  0.6 69.0 %copy-start.5 = (s32[4096]{0:T(1024)S(1)}, s32[4096]{0:T(1024)}, u32[]{:S(2)}) copy-start(s32[4096]{0:T(1024)} %param.19) | copy-start | bytes 49156
  0.6 69.0 %copy-start.8 = (f32[36]{0:T(128)S(1)}, f32[36]{0:T(128)}, u32[]{:S(2)}) copy-start(f32[36]{0:T(128)} %param.24) | copy-start | bytes 436
  0.7 69.0 %copy-start.6 = (f32[4,36]{1,0:T(4,128)S(1)}, f32[4,36]{1,0:T(4,128)}, u32[]{:S(2)}) copy-start(f32[4,36]{1,0:T(4,128)} %param.23) | copy-start | bytes 1732
  0.7 69.0 %copy-start.7 = (f32[4,36]{1,0:T(4,128)S(1)}, f32[4,36]{1,0:T(4,128)}, u32[]{:S(2)}) copy-start(f32[4,36]{1,0:T(4,128)} %param.25) | copy-start | bytes 1732
  0.7 69.1 %copy-start.4 = (f32[2048]{0:T(1024)S(1)}, f32[2048]{0:T(1024)}, u32[]{:S(2)}) copy-start(f32[2048]{0:T(1024)} %param.18) | copy-start | bytes 24580
  0.7 69.1 %copy-start.1 = (s32[4096]{0:T(1024)S(1)}, s32[4096]{0:T(1024)}, u32[]{:S(2)}) copy-start(s32[4096]{0:T(1024)} %param.20) | copy-start | bytes 49156
  0.7 69.1 %copy-start.2 = (s32[4096]{0:T(1024)S(1)}, s32[4096]{0:T(1024)}, u32[]{:S(2)}) copy-start(s32[4096]{0:T(1024)} %param.21) | copy-start | bytes 49156
  0.7 69.1 %copy-start.3 = (f32[4096]{0:T(1024)S(1)}, f32[4096]{0:T(1024)}, u32[]{:S(2)}) copy-start(f32[4096]{0:T(1024)} %param.22) | copy-start | bytes 49156
  69.8 0.9 %copy-start = (f32[16,2048]{1,0:T(8,128)S(1)}, f32[16,2048]{1,0:T(8,128)}, u32[]{:S(2)}) copy-start(f32[16,2048]{1,0:T(8,128)} %shard_map.148.cond_ref) | copy-start | bytes 393220

commit v2 on v1

--- a/solution.py
+++ b/solution.py
@@ -94,6 +94,7 @@
     k = 16 // rows_o
     mw = gw // k
     total_steps = groups * steps
+    cols_all = total_steps * tw
 
     barrier = pltpu.get_barrier_semaphore()
     for j in range(1, n_site):
@@ -191,15 +192,29 @@
     for s in range(per):
         xy_col[s * ns : (s + 1) * ns, :] = xy_rows[s].T
 
-    for j in range(1, n_real):
-        innov_copy(j).wait_recv()
-
     east = xy_ref[0:1, :] * COORD_SCALE
     north = xy_ref[1:2, :] * COORD_SCALE
     kt = math.gcd(ns, 256)
     k_count = ns // kt
-    pieces = tw // 16
+    pieces = tw // 32
+    early = cols_all // 2
+
+    def cross_piece(row):
+        row = pl.multiple_of(row, 16)
+        dx = xy_col[pl.ds(row, 16), 0:1] - east
+        dy = xy_col[pl.ds(row, 16), 1:2] - north
+        d2 = jnp.maximum(dx * dx + dy * dy, 1e-20)
+        cross[pl.ds(row, 16), :] = jnp.exp2(-(d2 * lax.rsqrt(d2))).astype(BF16)
+
+    def early_pieces(n, carry):
+        for m in range(8):
+            cross_piece(n * 128 + m * 16)
+        return carry
+
+    lax.fori_loop(0, early // 128, early_pieces, 0)
     acc[...] = jnp.zeros_like(acc)
+    for j in range(1, n_real):
+        innov_copy(j).wait_recv()
 
     def part_copy(g, j):
         peer = lax.rem(me_s + j, n_site)
@@ -272,11 +287,7 @@
             )
             upto = (p + 1) * pieces // k_count
             for m in range(done, upto):
-                row = pl.multiple_of(c * tw + m * 16, 16)
-                dx = xy_col[pl.ds(row, 16), 0:1] - east
-                dy = xy_col[pl.ds(row, 16), 1:2] - north
-                d2 = jnp.maximum(dx * dx + dy * dy, 1e-20)
-                cross[pl.ds(row, 16), :] = jnp.exp2(-(d2 * lax.rsqrt(d2))).astype(BF16)
+                cross_piece(early + c * (tw // 2) + m * 16)
             done = upto
         product = product.reshape(n_real, 2, rr, tw)
         partial = (product[:, 0] + product[:, 1]).reshape(n_site, rows_o, tw)
@@ -329,8 +340,8 @@
         for j in range(1, n_real):
             back_copy(j, n).start()
 
+    sum_and_share(groups - 1)
     apply_group(groups - 2, 512, lambda n: None)
-    sum_and_share(groups - 1)
     apply_group(groups - 1, bw, send_back)
 
     own_row = pl.multiple_of(me_r * rr, 8)
@@ -497,7 +508,7 @@
     reals = rr * n_real
     per = n_site // n_real
     tw = 256
-    groups = 5
+    groups = 4
     steps = cols // groups // tw
     nbuf = min(6, groups * steps)
     gw = tw * steps

time: 87 us -> 84.1 us (0.967)
  Pallas kernels: 80.3 us -> 77.4 us
    pallas_call x1, Pallas kernels: 66.2 us -> 63.5 us  [shards(): pl.pallas_call(functools.partial(krige_kernel, n_site, n_real, groups, st...]
where the time goes in v2:
time: 84.1 us; the launch traced here: 83.8 us
  Pallas kernels  77.4 us (92%)
  local copies, waits for them, and re-layouts  4.8 us (6%)
    pallas_call x1, Pallas kernels, shards(): pl.pallas_call(functools.partial(krige_kernel, n_site, n_real, groups, st...  63.5 us
    pallas_call x1, Pallas kernels, shards(): pl.pallas_call(functools.partial(loss_kernel, n_site, count * n_site), ou...  13.9 us
    unnamed x20, local copies, waits for them, and re-layouts  2.2 us

profile of v2, /device:TPU:0, one launch (start us, length us, event | category | flops | bytes accessed | tf_op | source)
XLA Modules:
  0.0 83.8 jit_solution(14679098577560613113)
XLA Ops:
  0.6 0.0 copy-start.5
  0.6 0.0 copy-start.8
  0.7 0.0 copy-start.6
  0.7 0.0 copy-start.7
  0.7 0.0 copy-start.4
  0.7 0.0 copy-start.1
  0.7 0.0 copy-start.2
  0.7 0.0 copy-start.3
  0.7 0.8 broadcast_subtract_fusion.1
  1.5 0.6 reshape.28.local_ref
  2.1 1.3 %reshape.27.observed_ref = f32[1,2560]{1,0:T(1,128)} reshape(f32[2560]{0:T(1024)} %param.14) | data formatting | bytes 20480 | tf_op jit(solution)/shard_map/reshape | solution.py:556
  3.4 63.5 %shard_map.148.cond_ref = f32[16,2048]{1,0:T(8,128)} custom-call(f32[16,2048]{1,0:T(8,128)} %field_ref.1, f32[1,2560]{1,0:T(1,128)} %reshape.27.observed_ref, f32[2560,5120]{1,0:T(8,128)} %inv_ref.1, f32[2,2048]{1,0:T(2,128)} %xy_ref.1, s32[1,2560]{1,0:T(1,128)} %reshape.28.local_ref), custom_call_target="tpu_custom_call" | custom-call | tf_op jit(solution)/shard_map/pallas_call | solution.py:521
  66.9 0.0 copy-done.5
  67.0 0.0 copy-done.8
  67.0 0.0 copy-done.6
  67.0 0.0 copy-done.7
  67.1 0.0 copy-done.4
  67.1 0.0 copy-done.1
  67.1 0.0 copy-done.2
  67.1 0.0 copy-done.3
  67.1 0.0 copy-start
  67.1 0.9 %copy-done = f32[16,2048]{1,0:T(8,128)S(1)} copy-done((f32[16,2048]{1,0:T(8,128)S(1)}, f32[16,2048]{1,0:T(8,128)}, u32[]{:S(2)}) %copy-start) | copy-done | bytes 131096
  68.0 13.9 %shard_map.149 = (f32[16,512]{1,0:T(8,128)S(1)}, f32[16,128]{1,0:T(8,128)S(1)}) custom-call(f32[16,2048]{1,0:T(8,128)S(1)} %copy-done, f32[1,2048]{1,0:T(1,128)S(1)} %bitcast.10, s32[1,4096]{1,0:T(1,128)S(1)} %bitcast.6, s32[1,4096]{1,0:T(1,128)S(1)} %bitcast.7, s32[1,4096]{1,0:T(1,128)S(1)} %bitcast.8, f32[1,4096]{1,0:T(1,128)S(1)} %bitcast.9, ...), custom_call_target="tpu_custom_call" | custom-call | tf_op jit(solution)/shard_map/pallas_call | solution.py:567
  81.9 0.6 slice_reduce_fusion
  82.5 0.7 copy.18
  83.1 0.6 copy.19
  (5 shorter events, 0.1 us)
Async XLA Ops:
  0.6 66.3 %copy-start.5 = (s32[4096]{0:T(1024)S(1)}, s32[4096]{0:T(1024)}, u32[]{:S(2)}) copy-start(s32[4096]{0:T(1024)} %param.19) | copy-start | bytes 49156
  0.6 66.3 %copy-start.8 = (f32[36]{0:T(128)S(1)}, f32[36]{0:T(128)}, u32[]{:S(2)}) copy-start(f32[36]{0:T(128)} %param.24) | copy-start | bytes 436
  0.7 66.3 %copy-start.6 = (f32[4,36]{1,0:T(4,128)S(1)}, f32[4,36]{1,0:T(4,128)}, u32[]{:S(2)}) copy-start(f32[4,36]{1,0:T(4,128)} %param.23) | copy-start | bytes 1732
  0.7 66.3 %copy-start.7 = (f32[4,36]{1,0:T(4,128)S(1)}, f32[4,36]{1,0:T(4,128)}, u32[]{:S(2)}) copy-start(f32[4,36]{1,0:T(4,128)} %param.25) | copy-start | bytes 1732
  0.7 66.4 %copy-start.4 = (f32[2048]{0:T(1024)S(1)}, f32[2048]{0:T(1024)}, u32[]{:S(2)}) copy-start(f32[2048]{0:T(1024)} %param.18) | copy-start | bytes 24580
  0.7 66.4 %copy-start.1 = (s32[4096]{0:T(1024)S(1)}, s32[4096]{0:T(1024)}, u32[]{:S(2)}) copy-start(s32[4096]{0:T(1024)} %param.20) | copy-start | bytes 49156
  0.7 66.4 %copy-start.2 = (s32[4096]{0:T(1024)S(1)}, s32[4096]{0:T(1024)}, u32[]{:S(2)}) copy-start(s32[4096]{0:T(1024)} %param.21) | copy-start | bytes 49156
  0.7 66.4 %copy-start.3 = (f32[4096]{0:T(1024)S(1)}, f32[4096]{0:T(1024)}, u32[]{:S(2)}) copy-start(f32[4096]{0:T(1024)} %param.22) | copy-start | bytes 49156
  67.1 0.9 %copy-start = (f32[16,2048]{1,0:T(8,128)S(1)}, f32[16,2048]{1,0:T(8,128)}, u32[]{:S(2)}) copy-start(f32[16,2048]{1,0:T(8,128)} %shard_map.148.cond_ref) | copy-start | bytes 393220
